TPU v7x, 32 devices: a whole 2x2x4 slice. The times are simulated.
32 devices in a mesh: mic: 8 (over z, y), mode: 4 (over x, core).
Axes of the slice: x: 2, y: 2, z: 4, core: 2. Of those that a mesh axis runs over, the one named last changes fastest.
Arguments:
- signal: bfloat16 [8, 2048, 4096], P('mic', 'mode'), may hold values from -6 to 6
- mic_axial: int32 [2048], P('mic'), may hold values from 0 to 63
- mic_azimuth: int32 [2048], P('mic'), may hold values from 0 to 511
- mode_m: int32 [8192], P('mode'), may hold values from -128 to 127
- mode_n: int32 [8192], P('mode'), may hold values from 0 to 31
- freq_bins: int32 [16], replicated, may hold values from 1 to 1023
Outputs:
- amplitude: float32 [16, 2, 8, 8192], P(None, None, None, 'mode')
- power: float32 [16, 8192], P(None, 'mode')
- residual: float32 [16, 2, 8, 2048], P('mode', None, None, 'mic')
All inputs are finite; a program needn't handle non-finite values.
Results may differ from a plain program's by a relative error of at most 0.0051.
Values may be sent and summed in bfloat16 or wider, within the bound.
A program may use at most 64 MiB of HBM per device.

v0:
```python
import math

import jax
import jax.numpy as jnp
from jax import lax
from jax.sharding import PartitionSpec as P

ITERS = 2
AZIM = 512
AXIAL = 64
NRAD = 32


EPS = 1e-06


def analysis_rows(freq_bins, seglen):
    sample_index = jnp.arange(seglen, dtype=jnp.int32)
    phase_turns = jnp.mod(freq_bins[:, None] * sample_index[None, :], seglen)
    phase_angle = phase_turns.astype(jnp.float32) * (2.0 * math.pi / seglen)
    window = 0.5 - 0.5 * jnp.cos(sample_index.astype(jnp.float32) * (2.0 * math.pi / seglen))
    norm_scale = (3.0 * seglen / 8.0) ** (-0.5)
    cosine = window[None, :] * jnp.cos(phase_angle) * norm_scale
    sine = -window[None, :] * jnp.sin(phase_angle) * norm_scale
    stacked = jnp.stack([cosine, sine], axis=1)
    return stacked.reshape(2 * freq_bins.shape[0], seglen).astype(jnp.bfloat16)


def mode_tile(bin_value, mic_axial, mic_azimuth, mode_m, mode_n, norm_scale):
    period = AZIM * AXIAL
    phase_turns = jnp.mod(
        mic_azimuth[:, None] * (mode_m * AXIAL)[None, :]
        + mic_axial[:, None] * (bin_value * (2 * NRAD - mode_n))[None, :],
        period,
    )
    phase_angle = phase_turns.astype(jnp.float32) * (2.0 * math.pi / period)
    weight = norm_scale / jnp.sqrt(1.0 + mode_n.astype(jnp.float32))
    real_part = (weight[None, :] * jnp.cos(phase_angle)).astype(jnp.bfloat16)
    imag_part = (weight[None, :] * jnp.sin(phase_angle)).astype(jnp.bfloat16)
    return (real_part, imag_part)


def forward_product(real_part, imag_part, vector):
    segs = vector.shape[1]
    stacked = vector.reshape(2 * segs, vector.shape[2]).astype(jnp.bfloat16)
    dims = (((1,), (1,)), ((), ()))
    first = lax.dot_general(stacked, real_part, dims, preferred_element_type=jnp.float32)
    second = lax.dot_general(stacked, imag_part, dims, preferred_element_type=jnp.float32)
    return jnp.stack([first[:segs] - second[segs:], first[segs:] + second[:segs]])


def adjoint_product(real_part, imag_part, vector):
    segs = vector.shape[1]
    stacked = vector.reshape(2 * segs, vector.shape[2]).astype(jnp.bfloat16)
    first = jnp.dot(stacked, real_part, preferred_element_type=jnp.float32)
    second = jnp.dot(stacked, imag_part, preferred_element_type=jnp.float32)
    return jnp.stack([first[:segs] + second[segs:], first[segs:] - second[:segs]])


def on_device(signal, mic_axial, mic_azimuth, mode_m, mode_n, freq_bins):
    seglen = signal.shape[2]
    freqs = freq_bins.shape[0]
    total_mics = mic_axial.shape[0] * lax.axis_size("mic")
    norm_scale = total_mics ** (-0.5)
    analysis = analysis_rows(freq_bins, seglen)
    spectra = lax.dot_general(
        analysis, signal, (((1,), (2,)), ((), ())), preferred_element_type=jnp.float32
    )
    spectra = spectra.reshape(freqs, 2, signal.shape[0], signal.shape[1])
    rhs = lax.all_to_all(
        lax.all_to_all(spectra, "mode", split_axis=0, concat_axis=3, tiled=True),
        "mic",
        split_axis=3,
        concat_axis=2,
        tiled=True,
    )
    freq_rows = rhs.shape[0]
    row_offset = lax.axis_index("mode") * freq_rows

    def tile_for(freq_row):
        bin_value = lax.dynamic_index_in_dim(freq_bins, freq_row, 0, keepdims=False)
        return mode_tile(bin_value, mic_axial, mic_azimuth, mode_m, mode_n, norm_scale)

    def gradients(residual_rows):

        def gradients_single(item):
            freq_row, vector = item
            real_part, imag_part = tile_for(freq_row)
            return adjoint_product(real_part, imag_part, vector)

        row_index = jnp.arange(residual_rows.shape[0], dtype=jnp.int32)
        return lax.map(gradients_single, (row_index, residual_rows))

    def gradient_of(residual):
        partial_sum = gradients(residual)
        gradient = lax.psum(partial_sum, "mic")
        grad_norm = lax.psum(jnp.sum(gradient * gradient, axis=(1, 3)), "mode")
        return (gradient, grad_norm)

    residual = lax.all_gather(rhs, "mode", axis=0, tiled=True)
    gradient, grad_norm = gradient_of(residual)
    direction = gradient
    amplitude = jnp.zeros_like(direction)
    for sweep in range(ITERS):

        def images_single(freq_row):
            real_part, imag_part = tile_for(freq_row)
            vector = lax.dynamic_index_in_dim(direction, freq_row, 0, keepdims=False)
            return forward_product(real_part, imag_part, vector)

        image = lax.psum(lax.map(images_single, jnp.arange(freqs, dtype=jnp.int32)), "mode")
        image_norm = lax.psum(jnp.sum(image * image, axis=(1, 3)), "mic")
        step_size = grad_norm / (image_norm + EPS)
        residual = residual - step_size[:, None, :, None] * image
        amplitude = amplitude + step_size[:, None, :, None] * direction
        if sweep + 1 < ITERS:
            gradient, next_norm = gradient_of(residual)
            momentum = next_norm / (grad_norm + EPS)
            direction = gradient + momentum[:, None, :, None] * direction
            grad_norm = next_norm
    residual_out = lax.dynamic_slice_in_dim(residual, row_offset, freq_rows, 0)
    power = jnp.mean(jnp.sum(amplitude * amplitude, axis=1), axis=1)
    return (amplitude, power, residual_out)


def solution(mesh):
    in_specs = (P("mic", "mode", None), P("mic"), P("mic"), P("mode"), P("mode"), P())
    out_specs = (P(None, None, None, "mode"), P(None, "mode"), P("mode", None, None, "mic"))
    return jax.shard_map(
        on_device, mesh=mesh, in_specs=in_specs, out_specs=out_specs, check_vma=False
    )
```

profile of v0, /device:TPU:0, one launch (start us, length us, event | category | flops | bytes accessed | tf_op | source)
XLA Modules:
  0.0 1672.1 jit_solution(18694547046799912)
XLA Ops:
  12.8 8.1 all_to_all.30
  50.2 329.9 %while.48 = (s32[]{:T(128)}, f32[16,2,8,2048]{3,2,1,0:T(8,128)S(1)}, bf16[16,2,8,256]{3,2,1,0:T(8,128)(2,1)S(1)}, f32[1,2048]{1,0:T(1,128)S(1)}, s32[256]{0:T(25...) while((s32[]{:T(128)}, ...), condition=%wide.region_1.2_spmd, body=%wide.region_0.1_spmd.sunk | while | flops 52504580 | bytes 1036487 | solution.py:92
  82.1 8.0 fusion.120
  102.0 8.0 fusion.120
  121.8 8.0 fusion.120
  141.7 8.0 fusion.120
  161.5 8.0 fusion.120
  181.4 8.0 fusion.120
  201.3 8.0 fusion.120
  221.1 8.0 fusion.120
  241.0 8.0 fusion.120
  260.9 8.0 fusion.120
  280.7 8.0 fusion.120
  300.6 8.0 fusion.120
  320.4 8.0 fusion.120
  340.3 8.0 fusion.120
  360.2 8.0 fusion.120
  381.6 98.6 %all-reduce.5.cloned.1.call-done = f32[16,2,8,2048]{3,2,1,0:T(8,128)} async-done(((f32[16,2,8,2048]{3,2,1,0:T(8,128)}), f32[16,2,8,2048]{3,2,1,0:T(8,128)}) %all-reduce.5.cloned.1.call-update) | async-done | bytes 2097168 | tf_op jit(solution)/shard_map/psum | solution.py:96
  482.7 318.0 %while.49 = (s32[]{:T(128)}, f32[16,2,8,256]{3,2,1,0:T(8,128)S(1)}, s32[16]{0:T(128)S(1)}, bf16[16,2,8,2048]{3,2,1,0:T(8,128)(2,1)S(1)}, f32[1,2048]{1,0:T(1,128...) while((s32[]{:T(128)}, f32[16,2,8,256]{3,2,1,0:T(8,128)S(1)}, ...), condition=%wide.region_6.7_spmd, body=%wide.region_5.6_spmd.sunk | while | flops 52447236 | bytes 348359 | solution.py:111
  494.5 8.0 fusion.126
  514.3 8.0 fusion.126
  534.2 8.0 fusion.126
  554.0 8.0 fusion.126
  573.9 8.0 fusion.126
  593.7 8.0 fusion.126
  613.6 8.0 fusion.126
  633.4 8.0 fusion.126
  653.3 8.0 fusion.126
  673.1 8.0 fusion.126
  692.9 8.0 fusion.126
  712.8 8.0 fusion.126
  732.6 8.0 fusion.126
  752.5 8.0 fusion.126
  772.3 8.0 fusion.126
  792.2 8.0 fusion.126
  807.9 25.4 %all-reduce.7.cloned.1.call-done = f32[16,2,8,256]{3,2,1,0:T(8,128)} async-done(((f32[16,2,8,256]{3,2,1,0:T(8,128)}), f32[16,2,8,256]{3,2,1,0:T(8,128)}) %all-reduce.7.cloned.1.call-update) | async-done | bytes 262160 | tf_op jit(solution)/shard_map/psum | solution.py:111
  834.3 21.6 %psum.59 = f32[16,8]{1,0:T(8,128)S(1)} all-reduce(f32[16,8]{1,0:T(8,128)S(1)} %multiply_reduce_fusion.4), channel_id=1, replica_groups=mesh['mic'=8,'mode'=4] {'mic'}, use_global_device_ids=true, to_apply=%region_9.10 | all-reduce | flops 128 | bytes 1024 | tf_op jit(solution)/shard_map/psum | solution.py:112
  857.9 317.9 %while.50 = (s32[]{:T(128)}, f32[16,2,8,2048]{3,2,1,0:T(8,128)S(1)}, bf16[16,2,8,256]{3,2,1,0:T(8,128)(2,1)S(1)}, f32[1,2048]{1,0:T(1,128)S(1)}, s32[256]{0:T(25...) while((s32[]{:T(128)}, ...), condition=%wide.region_11.12_spmd, body=%wide.region_10.11_spmd.sunk | while | flops 52504580 | bytes 1036487 | solution.py:92
  869.7 8.0 fusion.132
  889.6 8.0 fusion.132
  909.4 8.0 fusion.132
  929.3 8.0 fusion.132
  949.1 8.0 fusion.132
  1167.6 8.0 fusion.132
  1177.3 98.1 %all-reduce.9.cloned.1.call-done = f32[16,2,8,2048]{3,2,1,0:T(8,128)} async-done(((f32[16,2,8,2048]{3,2,1,0:T(8,128)}), f32[16,2,8,2048]{3,2,1,0:T(8,128)}) %all-reduce.9.cloned.1.call-update) | async-done | bytes 2097168 | tf_op jit(solution)/shard_map/psum | solution.py:96
  1287.1 317.5 %while.51 = (s32[]{:T(128)}, f32[16,2,8,256]{3,2,1,0:T(8,128)S(1)}, s32[16]{0:T(128)S(1)}, bf16[16,2,8,2048]{3,2,1,0:T(8,128)(2,1)S(1)}, f32[1,2048]{1,0:T(1,128...) while((s32[]{:T(128)}, f32[16,2,8,256]{3,2,1,0:T(8,128)S(1)}, ...), condition=%wide.region_16.17_spmd, body=%wide.region_15.16_spmd.sunk | while | flops 52447236 | bytes 348359 | solution.py:111
  1298.9 8.0 fusion.138
  1318.8 8.0 fusion.138
  1338.6 8.0 fusion.138
  1358.4 8.0 fusion.138
  1378.3 8.0 fusion.138
  1398.1 8.0 fusion.138
  1418.0 8.0 fusion.138
  1437.8 8.0 fusion.138
  1457.7 8.0 fusion.138
  1477.5 8.0 fusion.138
  1497.4 8.0 fusion.138
  1517.2 8.0 fusion.138
  1537.1 8.0 fusion.138
  1556.9 8.0 fusion.138
  1576.8 8.0 fusion.138
  1596.6 8.1 fusion.138
  1605.4 31.5 %all-reduce.11.cloned.1.call-done = f32[16,2,8,256]{3,2,1,0:T(8,128)} async-done(((f32[16,2,8,256]{3,2,1,0:T(8,128)}), f32[16,2,8,256]{3,2,1,0:T(8,128)}) %all-reduce.11.cloned.1.call-update) | async-done | bytes 262160 | tf_op jit(solution)/shard_map/psum | solution.py:111
  1638.0 21.6 %psum.63 = f32[16,8]{1,0:T(8,128)S(1)} all-reduce(f32[16,8]{1,0:T(8,128)S(1)} %multiply_reduce_fusion.3), channel_id=1, replica_groups=mesh['mic'=8,'mode'=4] {'mic'}, use_global_device_ids=true, to_apply=%region_19.20 | all-reduce | flops 128 | bytes 1024 | tf_op jit(solution)/shard_map/psum | solution.py:112
  (526 shorter events, 786.8 us)
Async XLA Ops:
  20.9 10.9 copy-start.3
  25.9 12.7 all-to-all-start.1
  31.8 448.4 %all-reduce.5.cloned.1.call-start = ((), (), s32[]{:S(2)}) async-start(), calls=%async_computation.2 | async-start | bytes 4194304 | tf_op jit(solution)/shard_map/psum | solution.py:96
  43.2 6.9 copy-start.4
  43.3 6.9 copy-start.7
  43.3 6.9 copy-start.8
  43.3 6.9 copy-start.9
  380.2 1.3 copy-start.1
  381.5 451.7 %all-reduce.7.cloned.1.call-start = ((), (), s32[]{:S(2)}) async-start(), calls=%async_computation.3 | async-start | bytes 524288 | tf_op jit(solution)/shard_map/psum | solution.py:111
  800.7 0.7 copy-start.6
  801.4 474.0 %all-reduce.9.cloned.1.call-start = ((), (), s32[]{:S(2)}) async-start(), calls=%async_computation.4 | async-start | bytes 4194304 | tf_op jit(solution)/shard_map/psum | solution.py:96
  1175.9 1.3 copy-start.2
  1177.2 106.4 %copy-start = (f32[16,2,8,2048]{3,2,1,0:T(8,128)S(1)}, f32[16,2,8,2048]{3,2,1,0:T(8,128)}, u32[]{:S(2)}) copy-start(f32[16,2,8,2048]{3,2,1,0:T(8,128)} %all-reduce.5.cloned.1.call-done) | copy-start | bytes 6291460
  1177.2 459.7 %all-reduce.11.cloned.1.call-start = ((), (), s32[]{:S(2)}) async-start(), calls=%async_computation.5 | async-start | bytes 524288 | tf_op jit(solution)/shard_map/psum | solution.py:111
  1604.7 0.7 copy-start.5
Sparse Core Ops, SparseCore 0:
  381.6 98.4 all-reduce.4
  801.5 31.6 all-reduce.6
  1177.4 97.9 all-reduce.8
  1605.5 31.3 all-reduce.10
where the time goes:
time: 1670 us
  matrix products  1030 us (62%)
  waiting for transfers between devices  260 us (16%)
  loops' own time  140 us (8%)
  local copies, waits for them, and re-layouts  89.3 us (5%)
  blocking collectives  70 us (4%)
  other arithmetic  64.7 us (4%)
    dot_general x32, matrix products, forward_product(): lax.dot_general(stacked, imag_part, dims, preferred_element_type=jnp.floa...  257 us
    dot_general x32, matrix products, adjoint_product(): second = jnp.dot(stacked, imag_part, preferred_element_type=jnp.float32)  257 us
    dot_general x32, matrix products, adjoint_product(): first = jnp.dot(stacked, real_part, preferred_element_type=jnp.float32)  255 us
    dot_general x32, matrix products, forward_product(): lax.dot_general(stacked, real_part, dims, preferred_element_type=jnp.floa...  255 us
    psum x2, waiting for transfers between devices, gradient_of(): gradient = lax.psum(partial_sum, 'mic')  197 us
    another operation x2, loops' own time, gradients(): return lax.map(gradients_single, (row_index, residual_rows))  76.1 us
    another operation x2, loops' own time, on_device(): lax.map(images_single, jnp.arange(freqs, dtype=jnp.int32))  64.1 us
    psum x2, waiting for transfers between devices, on_device(): lax.psum(lax.map(images_single, jnp.arange(freqs, dtype=jnp.int32)), 'mode')  56.9 us
  transfers between devices with their start and end apart: 5, of which 5 were waited for; matrix products, arithmetic and copies ran while one was open for 0% of the time, Pallas kernels for 0%

commit v1 on v0

v1 whole, which is shorter than its diff:
```python
import functools
import math

import jax
import jax.numpy as jnp
from jax import lax
from jax.experimental import pallas as pl
from jax.experimental.pallas import tpu as pltpu
from jax.sharding import PartitionSpec as P

AZIM = 512
AXIAL = 64
NRAD = 32
ORDERS = 256
EPS = 1e-06
NT = (((1,), (1,)), ((), ()))
NN = (((1,), (0,)), ((), ()))


def cos_sin(turns, period):
    quarter = period // 4
    shifted = turns + quarter // 2
    quadrant = lax.shift_right_arithmetic(
        shifted, jnp.int32(quarter.bit_length() - 1)
    )
    rest = jnp.bitwise_and(shifted, quarter - 1) - quarter // 2
    x = rest.astype(jnp.float32) * (2.0 * math.pi / period)
    x2 = x * x
    c = 1.0 + x2 * (-0.5 + x2 * (1.0 / 24 + x2 * (-1.0 / 720 + x2 * (1.0 / 40320))))
    s = x * (1.0 + x2 * (-1.0 / 6 + x2 * (1.0 / 120 + x2 * (-1.0 / 5040 + x2 * (1.0 / 362880)))))
    odd = jnp.bitwise_and(quadrant, 1) == 1
    cos_flip = jnp.bitwise_and(quadrant + 1, 2) == 2
    sin_flip = jnp.bitwise_and(quadrant, 2) == 2
    cos_val = jnp.where(odd, s, c)
    sin_val = jnp.where(odd, c, s)
    return jnp.where(cos_flip, -cos_val, cos_val), jnp.where(sin_flip, -sin_val, sin_val)


def analysis_rows(freq_bins, seglen):
    sample_index = jnp.arange(seglen, dtype=jnp.int32)
    cosine, sine = cos_sin(freq_bins[:, None] * sample_index[None, :], seglen)
    wave, _ = cos_sin(sample_index, seglen)
    window = (0.5 - 0.5 * wave) * (3.0 * seglen / 8.0) ** (-0.5)
    stacked = jnp.stack([window[None, :] * cosine, -window[None, :] * sine], axis=1)
    return stacked.reshape(2 * freq_bins.shape[0], seglen).astype(jnp.bfloat16)


def solve_kernel(
    pairs, segs, chunk, bins_ref, az_ref, ax_ref, m_ref, n_ref, rhs_ref, amp_ref, res_ref,
    t_re, t_im, g_re, g_im, image_ref, hot_ref,
):
    mics = rhs_ref.shape[1]
    modes = m_ref.shape[1]
    half = pairs * NRAD
    scale = 1.0 / mics
    chunks = [pl.ds(at, chunk) for at in range(0, mics, chunk)]
    mode_chunks = [pl.ds(at, chunk) for at in range(0, modes, chunk)]

    orders = lax.broadcasted_iota(jnp.int32, (ORDERS, chunk), 0) - ORDERS // 2
    radial = lax.broadcasted_iota(jnp.int32, (NRAD, chunk), 0)
    for part in chunks:
        cosine, sine = cos_sin(orders * az_ref[:, part], AZIM)
        g_re[:, part] = cosine.astype(jnp.bfloat16)
        g_im[:, part] = sine.astype(jnp.bfloat16)
        for f in range(pairs // segs):
            cosine, sine = cos_sin(ax_ref[:, part] * ((2 * NRAD - radial) * bins_ref[f]), AZIM * AXIAL)
            for s in range(segs):
                rows = pl.ds((f * segs + s) * NRAD, NRAD)
                t_re[rows, part] = cosine
                t_im[rows, part] = sine
    count = jnp.zeros((NRAD, ORDERS), jnp.float32)
    for part in mode_chunks:
        hot = jnp.where(orders == m_ref[:, part], 1.0, 0.0).astype(jnp.bfloat16)
        hot_ref[:, part] = hot
        radial_hot = jnp.where(radial == n_ref[:, part], 1.0, 0.0).astype(jnp.bfloat16)
        count += lax.dot_general(radial_hot, hot, NT, preferred_element_type=jnp.float32)
    radial_col = lax.broadcasted_iota(jnp.int32, (NRAD, ORDERS), 0).astype(jnp.float32)
    gram = count * (scale / (1.0 + radial_col))
    gram = jnp.concatenate([gram] * pairs, axis=0)

    def adjoint(source):
        cos_sum = jnp.zeros((2 * half, ORDERS), jnp.float32)
        sin_sum = jnp.zeros((2 * half, ORDERS), jnp.float32)
        for part in chunks:
            re_rows, im_rows = [], []
            for p in range(pairs):
                rows = pl.ds(p * NRAD, NRAD)
                a, b = t_re[rows, part], t_im[rows, part]
                v, w = source[p : p + 1, part], source[pairs + p : pairs + p + 1, part]
                re_rows.append((a * v + b * w).astype(jnp.bfloat16))
                im_rows.append((a * w - b * v).astype(jnp.bfloat16))
            x = jnp.concatenate(re_rows + im_rows, axis=0)
            cos_sum += lax.dot_general(x, g_re[:, part], NT, preferred_element_type=jnp.float32)
            sin_sum += lax.dot_general(x, g_im[:, part], NT, preferred_element_type=jnp.float32)
        return cos_sum[:half] + sin_sum[half:], cos_sum[half:] - sin_sum[:half]

    def forward(grid_re, grid_im):
        h = jnp.concatenate([gram * grid_re, gram * grid_im], axis=0).astype(jnp.bfloat16)
        for part in chunks:
            c = lax.dot_general(h, g_re[:, part], NN, preferred_element_type=jnp.float32)
            s = lax.dot_general(h, g_im[:, part], NN, preferred_element_type=jnp.float32)
            z_re, z_im = c[:half] - s[half:], c[half:] + s[:half]
            for p in range(pairs):
                rows = pl.ds(p * NRAD, NRAD)
                a, b = t_re[rows, part], t_im[rows, part]
                zr, zi = z_re[p * NRAD : (p + 1) * NRAD], z_im[p * NRAD : (p + 1) * NRAD]
                image_ref[p : p + 1, part] = jnp.sum(a * zr - b * zi, axis=0, keepdims=True)
                image_ref[pairs + p : pairs + p + 1, part] = jnp.sum(a * zi + b * zr, axis=0, keepdims=True)

    def grid_norm(grid_re, grid_im):
        power = gram * (grid_re * grid_re + grid_im * grid_im)
        sums = [jnp.sum(power[p * NRAD : (p + 1) * NRAD], keepdims=True) for p in range(pairs)]
        return jnp.concatenate(sums, axis=0)

    def image_norm():
        power = jnp.sum(image_ref[...] * image_ref[...], axis=1, keepdims=True)
        return power[:pairs] + power[pairs:]

    def twice(column):
        return jnp.concatenate([column, column], axis=0)

    def per_row(column):
        return jnp.concatenate(
            [jnp.broadcast_to(column[p : p + 1], (NRAD, 1)) for p in range(pairs)], axis=0
        )

    grad_re, grad_im = adjoint(rhs_ref)
    norm = grid_norm(grad_re, grad_im)
    forward(grad_re, grad_im)
    step = norm / (image_norm() + EPS)
    res_ref[...] = rhs_ref[...] - twice(step) * image_ref[...]
    next_re, next_im = adjoint(res_ref)
    next_norm = grid_norm(next_re, next_im)
    momentum = per_row(next_norm / (norm + EPS))
    dir_re = next_re + momentum * grad_re
    dir_im = next_im + momentum * grad_im
    forward(dir_re, dir_im)
    last = next_norm / (image_norm() + EPS)
    res_ref[...] = res_ref[...] - twice(last) * image_ref[...]
    first_rows, last_rows = per_row(step), per_row(last)
    amp = jnp.concatenate(
        [first_rows * grad_re + last_rows * dir_re, first_rows * grad_im + last_rows * dir_im], axis=0
    ).astype(jnp.bfloat16)
    for part in mode_chunks:
        spread = lax.dot_general(amp, hot_ref[:, part], NN, preferred_element_type=jnp.float32)
        mask = radial == n_ref[:, part]
        rows = [
            jnp.sum(jnp.where(mask, spread[p * NRAD : (p + 1) * NRAD], 0.0), axis=0, keepdims=True)
            for p in range(2 * pairs)
        ]
        amp_ref[:, part] = jnp.concatenate(rows, axis=0).astype(amp_ref.dtype)


def solve(bins, az, ax, m, n, rhs, segs):
    pairs = rhs.shape[0] // 2
    mics, modes = rhs.shape[1], m.shape[1]
    vmem = pl.BlockSpec(memory_space=pltpu.VMEM)
    return pl.pallas_call(
        functools.partial(solve_kernel, pairs, segs, 512),
        out_shape=(
            jax.ShapeDtypeStruct((2 * pairs, modes), jnp.bfloat16),
            jax.ShapeDtypeStruct((2 * pairs, mics), jnp.float32),
        ),
        in_specs=[pl.BlockSpec(memory_space=pltpu.SMEM)] + [vmem] * 5,
        out_specs=(vmem, vmem),
        scratch_shapes=[
            pltpu.VMEM((pairs * NRAD, mics), jnp.float32),
            pltpu.VMEM((pairs * NRAD, mics), jnp.float32),
            pltpu.VMEM((ORDERS, mics), jnp.bfloat16),
            pltpu.VMEM((ORDERS, mics), jnp.bfloat16),
            pltpu.VMEM((2 * pairs, mics), jnp.float32),
            pltpu.VMEM((ORDERS, modes), jnp.bfloat16),
        ],
        compiler_params=pltpu.CompilerParams(vmem_limit_bytes=40 * 1024 * 1024),
    )(bins, az, ax, m, n, rhs)


def on_device(signal, mic_axial, mic_azimuth, mode_m, mode_n, freq_bins):
    seglen = signal.shape[2]
    segs = signal.shape[0]
    freqs = freq_bins.shape[0]
    own = freqs // lax.axis_size("mode")
    mic_code = lax.all_gather(mic_azimuth * AXIAL + mic_axial, "mic", axis=0, tiled=True)
    mode_code = lax.all_gather(
        (mode_m + ORDERS // 2) * NRAD + mode_n, "mode", axis=0, tiled=True
    )
    mics, modes = mic_code.shape[0], mode_code.shape[0]
    analysis = analysis_rows(freq_bins, seglen)
    spectra = lax.dot_general(
        analysis, signal, (((1,), (2,)), ((), ())), preferred_element_type=jnp.float32
    )
    spectra = spectra.reshape(freqs, 2, segs, signal.shape[1])
    rhs = lax.all_to_all(spectra, "mode", split_axis=0, concat_axis=3, tiled=True)
    rhs = rhs.transpose(1, 0, 2, 3).reshape(2 * own * segs, mics)
    bins = lax.dynamic_slice_in_dim(freq_bins, lax.axis_index("mode") * own, own)
    az = lax.shift_right_logical(mic_code, 6)[None, :]
    ax = jnp.bitwise_and(mic_code, AXIAL - 1)[None, :]
    m = (lax.shift_right_logical(mode_code, 5) - ORDERS // 2)[None, :]
    n = jnp.bitwise_and(mode_code, NRAD - 1)[None, :]
    amp, res = solve(bins, az, ax, m, n, rhs, segs)
    amp = amp.reshape(2, own, segs, modes)
    amp = lax.all_to_all(amp, "mode", split_axis=3, concat_axis=1, tiled=True)
    amp = lax.all_gather(amp, "mic", axis=2, tiled=True)
    res = lax.all_to_all(
        res.reshape(2, own, segs, mics), "mic", split_axis=3, concat_axis=2, tiled=True
    )
    weight = mics ** (-0.5) / jnp.sqrt(1.0 + mode_n.astype(jnp.float32))
    amplitude = amp.astype(jnp.float32).transpose(1, 0, 2, 3) * weight
    power = jnp.mean(jnp.sum(amplitude * amplitude, axis=1), axis=1)
    return (amplitude, power, res.transpose(1, 0, 2, 3))


def solution(mesh):
    in_specs = (P("mic", "mode", None), P("mic"), P("mic"), P("mode"), P("mode"), P())
    out_specs = (P(None, None, None, "mode"), P(None, "mode"), P("mode", None, None, "mic"))
    return jax.shard_map(
        on_device, mesh=mesh, in_specs=in_specs, out_specs=out_specs, check_vma=False
    )
```

time: 1670 us -> 150 us (0.09)
  matrix products: 1030 us -> 3.54 us
  waiting for transfers between devices: 260 us -> 22.9 us
  loops' own time: 140 us -> 0 us
  other arithmetic: 64.7 us -> 4.45 us
  local copies, waits for them, and re-layouts: 89.3 us -> 50 us
  blocking collectives: 70 us -> 34.2 us
    dot_general x128 -> x0, matrix products: 1020 us -> none  [the longest x32 257 us: forward_product(): lax.dot_general(stacked, imag_part, dims, preferred_element_type=jnp.floa...]
    psum x4 -> x0, waiting for transfers between devices: 254 us -> none  [the longest x2 197 us: gradient_of(): gradient = lax.psum(partial_sum, 'mic')]
    another operation x4 -> x0, loops' own time: 140 us -> none  [the longest x2 76.1 us: gradients(): return lax.map(gradients_single, (row_index, residual_rows))]
    dynamic_slice x129 -> x1, local copies, waits for them, and re-layouts: 75.1 us -> 0.08 us  [on_device(): lax.dynamic_slice_in_dim(freq_bins, lax.axis_index('mode') * own, own)]
    psum x4 -> x0, blocking collectives: 56.1 us -> none  [the longest x2 43.2 us: on_device(): image_norm = lax.psum(jnp.sum(image * image, axis=(1, 3)), 'mic')]
    mul x64 -> x2, other arithmetic: 41.5 us -> 0.27 us  [the longest x1 0.25 us: on_device(): amplitude = amp.astype(jnp.float32).transpose(1, 0, 2, 3) * weight]
    all_gather x1 -> x2, blocking collectives: 5.79 us -> 26.6 us  [the longest x1 21.4 us: on_device(): lax.all_gather(mic_azimuth * AXIAL + mic_axial, 'mic', axis=0, tiled=True)]
    unnamed x22 -> x17, local copies, waits for them, and re-layouts: 11.1 us -> 28.3 us
  transfers between devices with their start and end apart: 5 -> 3, of which waited for: 5 -> 2; matrix products, arithmetic and copies ran while one was open for 0% -> 7% of each run, Pallas kernels for 0% -> 0%
where the time goes in v1:
time: 150 us; the launch traced here: 149 us
  local copies, waits for them, and re-layouts  50 us (33%)
  blocking collectives  34.2 us (23%)
  waiting for transfers between devices  22.9 us (15%)
  between operations  14.2 us (9%)
  Pallas kernels  12.3 us (8%)
  starting transfers between devices  7.56 us (5%)
  other arithmetic  4.45 us (3%)
  matrix products  3.54 us (2%)
    unnamed x17, local copies, waits for them, and re-layouts  28.3 us
    all_gather x1, blocking collectives, on_device(): lax.all_gather(mic_azimuth * AXIAL + mic_axial, 'mic', axis=0, tiled=True)  21.4 us
    all_gather x1, waiting for transfers between devices, on_device(): amp = lax.all_gather(amp, 'mic', axis=2, tiled=True)  15.9 us
    pallas_call x1, Pallas kernels, solve(): pl.pallas_call(functools.partial(solve_kernel, pairs, segs, 512), out_sha...  12.3 us
    all_to_all x3, local copies, waits for them, and re-layouts, on_device(): amp = lax.all_to_all(amp, 'mode', split_axis=3, concat_axis=1, tiled=True)  10.6 us
    all_to_all x1, blocking collectives, on_device(): amp = lax.all_to_all(amp, 'mode', split_axis=3, concat_axis=1, tiled=True)  7.64 us
    reshape x2, local copies, waits for them, and re-layouts, on_device(): amp = amp.reshape(2, own, segs, modes)  7.12 us
    all_to_all x1, waiting for transfers between devices, on_device(): lax.all_to_all(res.reshape(2, own, segs, mics), 'mic', split_axis=3, conc...  7.01 us
  transfers between devices with their start and end apart: 3, of which 2 were waited for; matrix products, arithmetic and copies ran while one was open for 7% of the time, Pallas kernels for 0%

profile of v1, /device:TPU:0, one launch (start us, length us, event | category | flops | bytes accessed | tf_op | source)
XLA Modules:
  0.0 149.2 jit_solution(18153030379819942857)
XLA Ops:
  7.2 1.1 fusion.6
  8.3 0.0 copy-start.3
  8.3 0.0 copy-start.4
  8.3 0.0 copy-start.1
  8.3 0.0 copy-start.2
  8.3 0.0 copy-start.5
  8.3 3.5 %fusion.2 = f32[16,2,1,512]{3,0,1,2:T(8,128)S(1)} fusion(bf16[1,512,4096]{2,1,0:T(8,128)(2,1)} %param.6, bf16[16,1,4096]{2,0,1:T(8,128)(2,1)S(1)} %get-tuple-element.21, bf16[16,1,4096]{2,0,1:T(8,128)(2,1)S(1)} %get-tuple-element.20), kind=kOutput, calls=%fused_computation.4 | convolution fusion | flops 134348800 | bytes 4521984 | tf_op jit(solution)/shard_map/dot_general | solution.py:189
  11.9 0.7 copy.16
  12.6 4.2 %all-to-all-start = ((f32[16,2,1,512]{3,1,2,0:T(2,128)}), f32[16,2,1,512]{3,1,2,0:T(2,128)S(1)}, u32[]{:S(2)}, u32[]{:S(2)}) async-start(f32[16,2,1,512]{3,1,2,0:T(2,128)} %copy.16), calls=%async_computation | async-start | bytes 131072 | tf_op jit(solution)/shard_map/all_to_all | solution.py:193
  16.8 0.0 all-gather.3.cloned.1.call-start
  16.8 0.0 copy-done.3
  16.8 0.0 copy-done.4
  16.8 21.4 %all-gather = s32[8,1,256]{2,1,0:T(1,128)S(1)} all-gather(s32[1,1,256]{2,1,0:T(1,128)S(1)} %bitcast.47), channel_id=1, replica_groups=mesh['mic'=8,'mode'=4] {'mic'}, dimensions={0}, use_global_device_ids=true | all-gather | bytes 9216 | tf_op jit(solution)/shard_map/all_gather | solution.py:183
  38.2 0.0 copy-done.1
  38.2 0.0 copy-done.2
  38.2 5.2 %all_gather.10 = s32[8192]{0:T(1024)S(1)} all-gather(s32[2048]{0:T(1024)S(1)} %multiply_add_fusion.2), channel_id=1, replica_groups=mesh['mic'=8,'mode'=4] {'mode'}, dimensions={0}, use_global_device_ids=true | all-gather | bytes 40960 | tf_op jit(solution)/shard_map/all_gather | solution.py:184
  43.5 0.0 copy-done.5
  43.5 0.1 dynamic_slice.3.bins_ref
  43.5 0.0 all-to-all-done
  43.6 0.1 all_to_all.38
  43.7 12.3 %shard_map.85 = (bf16[8,8192]{1,0:T(8,128)(2,1)S(1)}, f32[8,2048]{1,0:T(8,128)S(1)}) custom-call(s32[4]{0:T(128)S(1)} %dynamic_slice.3.bins_ref, s32[1,2048]{1,0:T(1,128)S(1)} %bitcast.37, s32[1,2048]{1,0:T(1,128)S(1)} %bitcast.36, s32[1,8192]{1,0:T(1,128)S(1)} %bitcast.35, s32[1,8192]{1,0:T(1,128)S(1)} %bitcast.34, f32[8,2048]{1,0:T(8,128)S(1)} %reshape.273.rhs_ref), custom_call_target="tpu_custom_call" | custom-call | tf_op jit(solution)/shard_map/pallas_call | solution.py:158
  56.0 0.1 reshape.274
  56.0 7.1 %copy.18 = bf16[2,4,1,8192]{1,0,2,3:T(2,128)(2,1)} copy(bf16[2,4,1,8192]{3,1,0,2:T(4,128)(2,1)S(1)} %reshape.274) | data formatting | bytes 262144 | tf_op jit(solution)/shard_map/reshape | solution.py:201
  63.1 8.7 %reshape.285 = bf16[4,2,8192]{2,1,0:T(2,128)(2,1)S(1)} reshape(bf16[8192,1,2,4]{3,2,1,0:T(2,128)(2,1)} %bitcast.38) | data formatting | bytes 262144
  71.8 7.6 %all_to_all.48 = bf16[4,2,8192]{2,1,0:T(2,128)(2,1)S(1)} all-to-all(bf16[4,2,8192]{2,1,0:T(2,128)(2,1)S(1)} %reshape.285), channel_id=1, replica_groups=mesh['mic'=8,'mode'=4] {'mode'}, dimensions={0} | all-to-all | bytes 262144 | tf_op jit(solution)/shard_map/all_to_all | solution.py:202
  79.4 10.0 %reshape.286 = bf16[8192,1,2,4]{3,2,1,0:T(2,128)(2,1)} reshape(bf16[4,2,8192]{2,1,0:T(2,128)(2,1)S(1)} %all_to_all.48) | data formatting | bytes 262144
  89.5 9.7 %copy.25 = bf16[2,4,1,4,2048]{4,3,1,0,2:T(4,128)(2,1)S(1)} copy(bf16[2,4,1,4,2048]{1,0,4,3,2:T(2,128)(2,1)} %bitcast.39) | data formatting | bytes 262144 | tf_op jit(solution)/shard_map/all_to_all | solution.py:202
  99.2 0.2 copy.20
  99.4 0.7 copy.21
  100.1 0.0 all-gather.3.cloned.1.call-update
  100.1 1.1 copy.22
  101.2 3.8 %reshape.287 = f32[8,1,2048]{2,1,0:T(1,128)} reshape(f32[2048,1,2,4]{3,2,1,0:T(2,128)S(1)} %bitcast.40) | data formatting | bytes 131072
  105.0 3.4 %all-to-all-start.2 = ((f32[8,1,2048]{2,1,0:T(1,128)}), f32[8,1,2048]{2,1,0:T(1,128)S(1)}, u32[]{:S(2)}, u32[]{:S(2)}) async-start(f32[8,1,2048]{2,1,0:T(1,128)} %reshape.287), calls=%async_computation.2 | async-start | bytes 131072 | tf_op jit(solution)/shard_map/all_to_all | solution.py:204
  108.4 7.0 %all-to-all-done.2 = f32[8,1,2048]{2,1,0:T(1,128)S(1)} async-done(((f32[8,1,2048]{2,1,0:T(1,128)}), f32[8,1,2048]{2,1,0:T(1,128)S(1)}, u32[]{:S(2)}, u32[]{:S(2)}) %all-to-all-start.2) | async-done | bytes 65568 | tf_op jit(solution)/shard_map/all_to_all | solution.py:204
  115.4 0.5 broadcast.556
  115.9 0.8 reduce.1
  116.7 3.2 %reshape.288 = f32[2048,1,2,4]{3,2,1,0:T(2,128)S(1)} reshape(f32[8,2048]{1,0:T(8,128)S(1)} %reduce.1) | data formatting | bytes 131072
  120.0 1.4 copy.23
  121.4 15.9 %all-gather.3.cloned.1.call-done = bf16[2,16,8,2048]{3,1,0,2:T(8,128)(2,1)} async-done(((bf16[2,16,1,2048]{3,1,0,2:T(8,128)(2,1)}), bf16[2,16,8,2048]{3,1,0,2:T(8,128)(2,1)}) %all-gather.3.cloned.1.call-update) | async-done | bytes 1048592 | tf_op jit(solution)/shard_map/all_gather | solution.py:203
  137.3 0.0 copy-start
  137.3 1.6 %multiply_reduce_fusion = f32[16,2048]{1,0:T(8,128)S(1)} fusion(f32[2048]{0:T(1024)S(1)} %rsqrt_multiply_fusion, bf16[2,16,8,2048]{3,1,0,2:T(8,128)(2,1)} %all-gather.3.cloned.1.call-done), kind=kLoop, calls=%fused_computation.2 | loop fusion | flops 2064384 | bytes 1187840 | tf_op jit(solution)/shard_map/reduce_sum | solution.py:209
  138.9 0.7 broadcast_multiply_fusion
  139.5 0.0 copy-done
  139.5 0.2 multiply_bitcast_fusion
  139.8 2.5 %copy.24 = f32[16,2,8,2048]{3,2,1,0:T(8,128)} copy(f32[16,2,8,2048]{3,0,1,2:T(8,128)S(1)} %multiply_bitcast_fusion) | data formatting | bytes 4194304
  (9 shorter events, 0.2 us)
Async XLA Ops:
  8.3 8.5 %copy-start.3 = (s32[256]{0:T(256)S(1)}, s32[256]{0:T(256)}, u32[]{:S(2)}) copy-start(s32[256]{0:T(256)} %param.7) | copy-start | bytes 3076
  8.3 8.5 %copy-start.4 = (s32[256]{0:T(256)S(1)}, s32[256]{0:T(256)}, u32[]{:S(2)}) copy-start(s32[256]{0:T(256)} %param.8) | copy-start | bytes 3076
  8.3 29.9 %copy-start.1 = (s32[2048]{0:T(1024)S(1)}, s32[2048]{0:T(1024)}, u32[]{:S(2)}) copy-start(s32[2048]{0:T(1024)} %param.10) | copy-start | bytes 24580
  8.3 29.9 %copy-start.2 = (s32[2048]{0:T(1024)S(1)}, s32[2048]{0:T(1024)}, u32[]{:S(2)}) copy-start(s32[2048]{0:T(1024)} %param.9) | copy-start | bytes 24580
  8.3 35.1 %copy-start.5 = (s32[16]{0:T(128)S(1)}, s32[16]{0:T(128)}, u32[]{:S(2)}) copy-start(s32[16]{0:T(128)} %param.11) | copy-start | bytes 196
  12.6 31.0 %all-to-all-start = ((f32[16,2,1,512]{3,1,2,0:T(2,128)}), f32[16,2,1,512]{3,1,2,0:T(2,128)S(1)}, u32[]{:S(2)}, u32[]{:S(2)}) async-start(f32[16,2,1,512]{3,1,2,0:T(2,128)} %copy.16), calls=%async_computation | async-start | bytes 131072 | tf_op jit(solution)/shard_map/all_to_all | solution.py:193
  16.8 120.5 %all-gather.3.cloned.1.call-start = ((), (), s32[]{:S(2)}) async-start(), calls=%async_computation.3 | async-start | bytes 1179648 | tf_op jit(solution)/shard_map/all_gather | solution.py:203
  105.0 10.4 %all-to-all-start.2 = ((f32[8,1,2048]{2,1,0:T(1,128)}), f32[8,1,2048]{2,1,0:T(1,128)S(1)}, u32[]{:S(2)}, u32[]{:S(2)}) async-start(f32[8,1,2048]{2,1,0:T(1,128)} %reshape.287), calls=%async_computation.2 | async-start | bytes 131072 | tf_op jit(solution)/shard_map/all_to_all | solution.py:204
  137.3 2.3 %copy-start = (bf16[2,16,8,2048]{3,1,0,2:T(8,128)(2,1)S(1)}, bf16[2,16,8,2048]{3,1,0,2:T(8,128)(2,1)}, u32[]{:S(2)}) copy-start(bf16[2,16,8,2048]{3,1,0,2:T(8,128)(2,1)} %all-gather.3.cloned.1.call-done) | copy-start | bytes 3145732
Sparse Core Ops, SparseCore 0:
  100.2 37.0 all-gather.2
